TPU v7x, 32 devices: a whole 2x2x4 slice. The times are simulated.
32 devices in a mesh: dp: 2 (over y), expert: 16 (over z, x, core).
Axes of the slice: x: 2, y: 2, z: 4, core: 2. Of those that a mesh axis runs over, the one named last changes fastest.
Arguments:
- tokens: bfloat16 [512, 2048], P(('dp', 'expert')), may hold values from -6 to 6
- cotangent: bfloat16 [512, 2048], P(('dp', 'expert')), may hold values from -6 to 6
- gate_probs: float32 [512, 8], P(('dp', 'expert')), may hold values from 0.15 to 0.35
- expert_ids: int32 [512, 8], P(('dp', 'expert')), may hold values from 0 to 15, as said below
- up_weight: bfloat16 [16, 768, 2048], P('expert', 'dp'), may hold values from -0.125 to 0.125
- down_weight: bfloat16 [16, 768, 2048], P('expert', 'dp'), may hold values from -0.21875 to 0.21875
Outputs:
- mixture: bfloat16 [512, 2048], P(('dp', 'expert'))
- input_grad: bfloat16 [512, 2048], P(('dp', 'expert'))
- gate_grad: float32 [512, 8], P(('dp', 'expert'))
Inputs may be any that keep to these rules, and one draw needn't show every extreme that they name: `expert_ids`: the 8 experts of a row differ. The 16 rows of every device name one and the same expert exactly 9 times; they name every other expert at most 8 times, and one other expert exactly 8 times on every device.
All inputs are finite; a program needn't handle non-finite values.
Results may differ from a plain program's by a relative error of at most 0.0058.
Values may be sent and summed in bfloat16 or wider, within the bound.
A program may use at most 64 MiB of HBM per device.

v0:
```python
import jax
import jax.numpy as jnp
from jax import lax
from jax.sharding import PartitionSpec as P


def broadcast(block, axis, owner):
    block = jnp.where(lax.axis_index(axis) == owner, block, jnp.zeros_like(block))
    return lax.psum(block, axis)


def expert_terms(row_block, up_piece, down_piece):
    model_width = row_block.shape[1] // 2
    features = row_block[:, :model_width]
    row_grads = row_block[:, model_width:]
    pre_act = jnp.einsum("rd,hd->rh", features, up_piece, preferred_element_type=jnp.float32)
    gating = jax.nn.sigmoid(pre_act)
    hidden = (pre_act * gating).astype(jnp.bfloat16)
    output_rows = jnp.dot(hidden, down_piece, preferred_element_type=jnp.float32)
    hidden_grad = jnp.einsum("rd,hd->rh", row_grads, down_piece, preferred_element_type=jnp.float32)
    act_grad = (hidden_grad * gating * (1.0 + pre_act * (1.0 - gating))).astype(jnp.bfloat16)
    input_rows = jnp.dot(act_grad, up_piece, preferred_element_type=jnp.float32)
    return jnp.concatenate([output_rows, input_rows], 1)


def spread(up_parts, down_parts, row_sets):
    model_width = up_parts.shape[2]
    initial = tuple(
        (jnp.zeros((row_block.shape[0], 2 * model_width), jnp.float32) for row_block in row_sets)
    )
    up_piece = lax.all_gather(up_parts, "dp", axis=1, tiled=True)
    down_piece = lax.all_gather(down_parts, "dp", axis=1, tiled=True)
    return tuple(
        (
            expert_terms(row_block, up_piece[member], down_piece[member])
            for member, (running, row_block) in enumerate(zip(initial, row_sets))
        )
    )


def shards(tokens, cotangent, gate_probs, expert_ids, up_weight, down_weight):
    tok_rows, model_width = tokens.shape
    top_count = expert_ids.shape[1]
    experts = lax.axis_size("expert")
    hot_rows = 9 * tok_rows // 16
    cold_total = experts - 1
    capacity = (tok_rows * top_count - hot_rows + cold_total - 1) // cold_total
    flat_ids = expert_ids.reshape(-1)
    slot_count = flat_ids.shape[0]
    one_hot = (flat_ids[:, None] == jnp.arange(experts, dtype=jnp.int32)[None, :]).astype(jnp.int32)
    hottest = jnp.argmax(jnp.sum(one_hot, 0))
    before = jnp.cumsum(one_hot, 0) - one_hot
    slot_rank = jnp.sum(before * one_hot, 1)
    slot_total = experts * capacity + hot_rows
    slot_index = jnp.where(
        flat_ids == hottest, experts * capacity + slot_rank, flat_ids * capacity + slot_rank
    )
    source_slot = (
        jnp.full((slot_total,), slot_count, jnp.int32)
        .at[slot_index]
        .set(jnp.arange(slot_count, dtype=jnp.int32))
    )
    source_row = source_slot // top_count
    payload = jnp.concatenate([tokens, cotangent], 1)
    padded_payload = jnp.concatenate([payload, jnp.zeros((1, 2 * model_width), payload.dtype)], 0)
    placed = padded_payload[source_row]
    outgoing = placed[: experts * capacity].reshape(experts, capacity, 2 * model_width)
    local_rows = placed[experts * capacity :]
    arrived = lax.all_to_all(outgoing, "expert", split_axis=0, concat_axis=0, tiled=True)
    arrived_rows = arrived.reshape(experts * capacity, 2 * model_width)
    shadow_up, shadow_down = (
        broadcast(up_weight[0], "expert", hottest),
        broadcast(down_weight[0], "expert", hottest),
    )
    (own_out,) = spread(up_weight, down_weight, [arrived_rows])
    (hot_out,) = spread(shadow_up[None], shadow_down[None], [local_rows])
    returning = own_out.astype(jnp.bfloat16).reshape(experts, capacity, 2 * model_width)
    came_back = lax.all_to_all(returning, "expert", split_axis=0, concat_axis=0, tiled=True)
    results = jnp.concatenate(
        [came_back.reshape(experts * capacity, 2 * model_width), hot_out.astype(jnp.bfloat16)], 0
    )
    per_slot = results[slot_index].astype(jnp.float32).reshape(tok_rows, top_count, 2 * model_width)
    scale = gate_probs[:, :, None]
    mixture = jnp.sum(scale * per_slot[:, :, :model_width], 1).astype(jnp.bfloat16)
    input_grad = jnp.sum(scale * per_slot[:, :, model_width:], 1).astype(jnp.bfloat16)
    gate_grad = jnp.sum(cotangent.astype(jnp.float32)[:, None, :] * per_slot[:, :, :model_width], 2)
    return (mixture, input_grad, gate_grad)


def solution(mesh):
    placed = (
        P(("dp", "expert"), None),
        P(("dp", "expert"), None),
        P(("dp", "expert"), None),
        P(("dp", "expert"), None),
        P("expert", "dp", None),
        P("expert", "dp", None),
    )
    return jax.shard_map(
        shards,
        mesh=mesh,
        in_specs=placed,
        out_specs=(P(("dp", "expert"), None), P(("dp", "expert"), None), P(("dp", "expert"), None)),
        check_vma=False,
    )
```

profile of v0, /device:TPU:0, one launch (start us, length us, event | category | flops | bytes accessed | tf_op | source)
XLA Modules:
  0.0 228.9 jit_solution(13746618031160292747)
XLA Ops:
  8.0 0.0 copy-start.1
  8.0 0.0 all-reduce.4.cloned.1.call-start
  8.1 0.9 copy.18
  8.9 0.1 eq.37
  9.0 0.1 fusion.68
  9.1 0.2 reduce_window_sum.11
  9.3 0.2 select_reduce_fusion
  9.5 0.7 iota_reduce_fusion
  10.8 1.3 broadcast_select_fusion.1
  12.0 0.0 copy-done.1
  12.0 1.3 broadcast_select_fusion
  13.3 0.0 all-reduce.4.cloned.1.call-update
  13.3 0.0 copy-start.6
  13.3 0.0 copy-start.4
  13.3 0.0 copy-start.5
  13.4 0.0 all-gather.5.cloned.1.call-start
  13.4 0.5 all-gather.5.cloned.1.call-update
  13.9 0.0 all-gather.7.cloned.1.call-start
  14.0 0.5 all-gather.7.cloned.1.call-update
  14.5 0.0 all-gather.9.cloned.1.call-start
  14.6 0.0 copy-done.6
  14.6 0.7 broadcast_compare_fusion
  15.2 0.1 copy.19
  15.3 0.1 eq.43
  15.4 0.1 copy.20
  15.5 0.1 mul.69
  15.6 1.0 scatter_custom_fusion
  16.6 103.3 %all-reduce.4.cloned.1.call-done = (bf16[1,384,2048]{2,1,0:T(8,128)(2,1)}, bf16[1,384,2048]{2,1,0:T(8,128)(2,1)}) async-done(((bf16[1,384,2048]{2,1,0:T(8,128)(2,1)}, bf16[1,384,2048]{2,1,0:T(8,128)(2,1)}), (bf16[1,384,2048]{2,1,0:T(8,128)(2,1)}, bf16[1,384,2048]{2,1,0:T(8,128)(2,1)})) %all-reduce.4.cloned.1.call-update) | async-done | bytes 3145744 | tf_op jit(solution)/shard_map/psum | solution.py:9
  120.0 0.0 all-gather.9.cloned.1.call-update
  120.0 0.0 copy-done.4
  120.0 0.0 copy-done.5
  120.0 1.3 gather_fusion
  121.3 0.0 copy-start.2
  121.3 1.1 slice_bitcast_fusion
  122.5 3.7 %all-to-all-start = ((bf16[16,8,4096]{2,1,0:T(8,128)(2,1)}), bf16[16,8,4096]{2,1,0:T(8,128)(2,1)S(1)}, u32[]{:S(2)}, u32[]{:S(2)}) async-start(bf16[16,8,4096]{2,1,0:T(8,128)(2,1)} %slice_bitcast_fusion), calls=%async_computation | async-start | bytes 2097152 | tf_op jit(solution)/shard_map/all_to_all | solution.py:69
  126.1 0.0 all-gather.11.cloned.1.call-start
  126.2 0.7 all-gather.11.cloned.1.call-update
  126.9 22.2 %all-to-all-done = bf16[16,8,4096]{2,1,0:T(8,128)(2,1)S(1)} async-done(((bf16[16,8,4096]{2,1,0:T(8,128)(2,1)}), bf16[16,8,4096]{2,1,0:T(8,128)(2,1)S(1)}, u32[]{:S(2)}, u32[]{:S(2)}) %all-to-all-start) | async-done | bytes 1048608 | tf_op jit(solution)/shard_map/all_to_all | solution.py:69
  149.0 0.0 all-gather.5.cloned.1.call-done
  149.0 3.1 %fusion.14 = f32[128,768]{1,0:T(8,128)S(1)} fusion(bf16[1,768,2048]{2,1,0:T(8,128)(2,1)} %all-gather.5.cloned.1.call-done, bf16[128,4096]{1,0:T(8,128)(2,1)S(1)} %bitcast.73), kind=kOutput, calls=%fused_computation.17 | convolution fusion | flops 402653184 | bytes 4063232 | tf_op jit(solution)/shard_map/rd,hd->rh/dot_general | solution.py:16
  152.1 0.0 copy-start.3
  152.1 0.0 all-gather.7.cloned.1.call-done
  152.1 0.7 copy-done.3
  152.9 2.5 %fusion.16 = bf16[16,8,2048]{2,1,0:T(8,128)(2,1)S(1)} fusion(bf16[1,768,2048]{2,1,0:T(8,128)(2,1)} %all-gather.7.cloned.1.call-done, f32[128,768]{1,0:T(8,128)S(1)} %fusion.14), kind=kOutput, calls=%fused_computation.19 | convolution fusion | flops 403406848 | bytes 4063232 | tf_op jit(solution)/shard_map/dot_general | solution.py:19
  155.3 5.1 %fusion.19 = bf16[16,8,2048]{2,1,0:T(8,128)(2,1)S(1)} fusion(bf16[1,768,2048]{2,1,0:T(8,128)(2,1)} %all-gather.5.cloned.1.call-done, bf16[1,768,2048]{2,1,0:T(8,128)(2,1)} %all-gather.7.cloned.1.call-done, bf16[128,4096]{1,0:T(8,128)(2,1)S(1)} %bitcast.74, f32[128,768]{1,0:T(8,128)} %copy-done.3), kind=kOutput, calls=%fused_computation.20 | convolution fusion | flops 806453248 | bytes 7733248 | tf_op jit(solution)/shard_map/dot_general | solution.py:22
  160.4 0.0 copy-start.7
  160.4 1.0 pad_maximum_fusion
  161.5 6.9 %all-to-all-start.1 = ((bf16[16,8,4096]{2,1,0:T(8,128)(2,1)}), bf16[16,8,4096]{2,1,0:T(8,128)(2,1)}, u32[]{:S(2)}, u32[]{:S(2)}) async-start(bf16[16,8,4096]{2,1,0:T(8,128)(2,1)} %pad_maximum_fusion), calls=%async_computation.1 | async-start | bytes 2097152 | tf_op jit(solution)/shard_map/all_to_all | solution.py:78
  168.4 0.0 copy-done.7
  168.4 0.1 copy.17
  168.5 0.0 all-gather.9.cloned.1.call-done
  168.5 0.0 copy-done.2
  168.5 2.8 %fusion.6 = f32[9,768]{1,0:T(8,128)S(1)} fusion(bf16[1,768,2048]{2,1,0:T(8,128)(2,1)} %all-gather.9.cloned.1.call-done, bf16[137,4096]{1,0:T(8,128)(2,1)S(1)} %gather_fusion), kind=kOutput, calls=%fused_computation.9 | convolution fusion | flops 28311552 | bytes 3238912 | tf_op jit(solution)/shard_map/rd,hd->rh/dot_general | solution.py:16
  171.3 0.0 copy-start
  171.3 38.8 %all-gather.11.cloned.1.call-done = bf16[1,768,2048]{2,1,0:T(8,128)(2,1)} async-done(((bf16[1,384,2048]{2,1,0:T(8,128)(2,1)}), bf16[1,768,2048]{2,1,0:T(8,128)(2,1)}) %all-gather.11.cloned.1.call-update) | async-done | bytes 3145744 | tf_op jit(solution)/shard_map/all_gather | solution.py:32
  210.2 2.4 %fusion.25 = bf16[9,2048]{1,0:T(8,128)(2,1)S(1)} fusion(bf16[1,768,2048]{2,1,0:T(8,128)(2,1)} %all-gather.11.cloned.1.call-done, f32[9,768]{1,0:T(8,128)S(1)} %fusion.6), kind=kOutput, calls=%fused_computation.22 | convolution fusion | flops 28364544 | bytes 3210240 | tf_op jit(solution)/shard_map/dot_general | solution.py:19
  212.6 0.0 copy-done
  212.6 3.8 %fusion.22 = bf16[9,2048]{1,0:T(8,128)(2,1)S(1)} fusion(bf16[1,768,2048]{2,1,0:T(8,128)(2,1)S(1)} %copy-done, bf16[1,768,2048]{2,1,0:T(8,128)(2,1)} %all-gather.11.cloned.1.call-done, bf16[137,4096]{1,0:T(8,128)(2,1)} %copy-done.2, f32[9,768]{1,0:T(8,128)S(1)} %fusion.6), kind=kOutput, calls=%fused_computation.21 | convolution fusion | flops 56703744 | bytes 6421504 | tf_op jit(solution)/shard_map/dot_general | solution.py:22
  216.4 0.0 all-to-all-done.1
  216.4 1.3 maximum_maximum_fusion
  217.8 1.2 gather_fusion.1
  219.0 0.2 bitcast_convert_fusion
  219.2 1.4 fusion.49
  220.6 0.7 copy.21
  (8 shorter events, 0.1 us)
Async XLA Ops:
  8.0 4.0 %copy-start.1 = (bf16[1,384,2048]{2,1,0:T(8,128)(2,1)S(1)}, bf16[1,384,2048]{2,1,0:T(8,128)(2,1)}, u32[]{:S(2)}) copy-start(bf16[1,384,2048]{2,1,0:T(8,128)(2,1)} %param.11) | copy-start | bytes 4718596
  8.0 112.0 %all-reduce.4.cloned.1.call-start = ((), (), s32[]{:S(2)}) async-start(), calls=%async_computation.6 | async-start | bytes 6291456 | tf_op jit(solution)/shard_map/psum | solution.py:9
  13.3 1.3 copy-start.6
  13.3 106.7 %copy-start.4 = (bf16[16,2048]{1,0:T(8,128)(2,1)S(1)}, bf16[16,2048]{1,0:T(8,128)(2,1)}, u32[]{:S(2)}) copy-start(bf16[16,2048]{1,0:T(8,128)(2,1)} %param.7) | copy-start | bytes 196612
  13.3 106.7 %copy-start.5 = (bf16[16,2048]{1,0:T(8,128)(2,1)S(1)}, bf16[16,2048]{1,0:T(8,128)(2,1)}, u32[]{:S(2)}) copy-start(bf16[16,2048]{1,0:T(8,128)(2,1)} %param.6) | copy-start | bytes 196612
  13.4 135.7 %all-gather.5.cloned.1.call-start = ((), (), s32[]{:S(2)}) async-start(), calls=%async_computation.2 | async-start | bytes 4718592 | tf_op jit(solution)/shard_map/all_gather | solution.py:31
  13.9 138.2 %all-gather.7.cloned.1.call-start = ((), (), s32[]{:S(2)}) async-start(), calls=%async_computation.3 | async-start | bytes 4718592 | tf_op jit(solution)/shard_map/all_gather | solution.py:32
  14.5 154.0 %all-gather.9.cloned.1.call-start = ((), (), s32[]{:S(2)}) async-start(), calls=%async_computation.4 | async-start | bytes 4718592 | tf_op jit(solution)/shard_map/all_gather | solution.py:31
  121.3 47.2 %copy-start.2 = (bf16[137,4096]{1,0:T(8,128)(2,1)}, bf16[137,4096]{1,0:T(8,128)(2,1)S(1)}, u32[]{:S(2)}) copy-start(bf16[137,4096]{1,0:T(8,128)(2,1)S(1)} %gather_fusion) | copy-start | bytes 3366916
  122.5 26.6 %all-to-all-start = ((bf16[16,8,4096]{2,1,0:T(8,128)(2,1)}), bf16[16,8,4096]{2,1,0:T(8,128)(2,1)S(1)}, u32[]{:S(2)}, u32[]{:S(2)}) async-start(bf16[16,8,4096]{2,1,0:T(8,128)(2,1)} %slice_bitcast_fusion), calls=%async_computation | async-start | bytes 2097152 | tf_op jit(solution)/shard_map/all_to_all | solution.py:69
  126.1 84.0 %all-gather.11.cloned.1.call-start = ((), (), s32[]{:S(2)}) async-start(), calls=%async_computation.5 | async-start | bytes 4718592 | tf_op jit(solution)/shard_map/all_gather | solution.py:32
  152.1 0.7 copy-start.3
  160.4 8.0 %copy-start.7 = (f32[16,8]{0,1:T(8,128)S(1)}, f32[16,8]{0,1:T(8,128)}, u32[]{:S(2)}) copy-start(f32[16,8]{0,1:T(8,128)} %param.8) | copy-start | bytes 1540
  161.5 54.9 %all-to-all-start.1 = ((bf16[16,8,4096]{2,1,0:T(8,128)(2,1)}), bf16[16,8,4096]{2,1,0:T(8,128)(2,1)}, u32[]{:S(2)}, u32[]{:S(2)}) async-start(bf16[16,8,4096]{2,1,0:T(8,128)(2,1)} %pad_maximum_fusion), calls=%async_computation.1 | async-start | bytes 2097152 | tf_op jit(solution)/shard_map/all_to_all | solution.py:78
  171.3 41.2 %copy-start = (bf16[1,768,2048]{2,1,0:T(8,128)(2,1)S(1)}, bf16[1,768,2048]{2,1,0:T(8,128)(2,1)}, u32[]{:S(2)}) copy-start(bf16[1,768,2048]{2,1,0:T(8,128)(2,1)} %all-gather.9.cloned.1.call-done) | copy-start | bytes 9437188
Sparse Core Ops, SparseCore 0:
  13.4 106.4 all-reduce.3
Sparse Core Ops, SparseCore 1:
  15.4 47.5 all-gather.4
  64.3 44.8 all-gather.6
  120.1 43.7 all-gather.8
  165.4 44.7 all-gather.10
where the time goes:
time: 229 us
  waiting for transfers between devices  166 us (72%)
  matrix products  19.7 us (9%)
  between operations  16.6 us (7%)
  starting transfers between devices  10.8 us (5%)
  other arithmetic  8.34 us (4%)
  local copies, waits for them, and re-layouts  7.33 us (3%)
    psum x1, waiting for transfers between devices, broadcast(): return lax.psum(block, axis)  103 us
    all_gather x2, waiting for transfers between devices, spread(): down_piece = lax.all_gather(down_parts, 'dp', axis=1, tiled=True)  38.9 us
    all_to_all x1, waiting for transfers between devices, shards(): lax.all_to_all(outgoing, 'expert', split_axis=0, concat_axis=0, tiled=True)  22.2 us
    dot_general x2, matrix products, expert_terms(): input_rows = jnp.dot(act_grad, up_piece, preferred_element_type=jnp.float32)  8.94 us
    all_to_all x1, starting transfers between devices, shards(): lax.all_to_all(returning, 'expert', split_axis=0, concat_axis=0, tiled=True)  6.9 us
    dot_general x2, matrix products, expert_terms(): jnp.einsum('rd,hd->rh', features, up_piece, preferred_element_type=jnp.fl...  5.87 us
    dot_general x2, matrix products, expert_terms(): jnp.dot(hidden, down_piece, preferred_element_type=jnp.float32)  4.87 us
  transfers between devices with their start and end apart: 7, of which 3 were waited for; matrix products, arithmetic and copies ran while one was open for 11% of the time, Pallas kernels for 0%

commit v1 on v0

--- a/solution.py
+++ b/solution.py
@@ -1,6 +1,10 @@
+import functools
+
 import jax
 import jax.numpy as jnp
 from jax import lax
+from jax.experimental import pallas as pl
+from jax.experimental.pallas import tpu as pltpu
 from jax.sharding import PartitionSpec as P
 
 
@@ -87,7 +91,235 @@
     return (mixture, input_grad, gate_grad)
 
 
+MESH = pl.DeviceIdType.MESH
+LANES = 128
+Z, Y, X, C = 4, 2, 2, 2
+
+
+def exchange_kernel(
+    experts,
+    tokens_ref, cotangent_ref, gate_ref, ids_ref, up_hbm, down_hbm,
+    mixture_ref, input_grad_ref, gate_grad_ref,
+    up, down, gathered, partial, from_core, core_sum, from_first, first_sum, from_second, plane_sum, from_z,
+    load_sem, send_sem, recv_sem,
+):
+    width = tokens_ref.shape[1]
+    near = LANES + width
+    rows = tokens_ref.shape[0]
+    y, expert = lax.axis_index("dp"), lax.axis_index("expert")
+    z = expert // (X * C)
+    x = (expert // C) % X
+    c = expert % C
+    far_y, far_x, far_c = 1 - y, 1 - x, 1 - c
+
+    def place(yy, zz, xx, cc):
+        return (yy, (zz * X + xx) * C + cc)
+
+    by_x, by_y, by_c = place(y, z, far_x, c), place(far_y, z, x, c), place(y, z, x, far_c)
+    planes = [(z + step) % Z for step in range(Z)]
+
+    loads = [
+        pltpu.make_async_copy(up_hbm.at[0], up, load_sem.at[0]),
+        pltpu.make_async_copy(down_hbm.at[0], down, load_sem.at[1]),
+    ]
+    for load in loads:
+        load.start()
+
+    barrier = pltpu.get_barrier_semaphore()
+    partners = [by_x, by_y, by_c] + [place(y, planes[step], x, c) for step in range(1, Z)]
+    for partner in partners:
+        pl.semaphore_signal(barrier, inc=1, device_id=partner, device_id_type=MESH)
+
+    lane = lax.broadcasted_iota(jnp.int32, (rows, LANES), 1)
+    weights = jnp.zeros((rows, LANES), jnp.float32)
+    for k in range(gate_ref.shape[1]):
+        weights += jnp.where(lane == ids_ref[:, k : k + 1], gate_ref[:, k : k + 1], 0.0)
+    high = weights.astype(jnp.bfloat16).astype(jnp.float32)
+    rest = jnp.zeros((rows, LANES), jnp.float32)
+    for k in range(gate_ref.shape[1]):
+        gate = gate_ref[:, k : k + 1]
+        rest += jnp.where(
+            lane == ids_ref[:, k : k + 1] + experts,
+            gate - gate.astype(jnp.bfloat16).astype(jnp.float32),
+            0.0,
+        )
+    gathered[0, c, y, x, :, :LANES] = (high + rest).astype(jnp.bfloat16)
+    gathered[0, c, y, x, :, LANES:near] = tokens_ref[...]
+    gathered[0, c, y, x, :, near:] = cotangent_ref[...]
+    pl.semaphore_wait(barrier, len(partners))
+
+    started = []
+
+    def send(src, dst, device):
+        index = len(started)
+        copy = pltpu.make_async_remote_copy(
+            src_ref=src, dst_ref=dst, send_sem=send_sem.at[index], recv_sem=recv_sem.at[index],
+            device_id=device, device_id_type=MESH,
+        )
+        copy.start()
+        started.append(copy)
+        return copy
+
+    first_cols, second_cols = pl.ds(0, near), pl.ds(near, width)
+    pending = {}
+    for step in range(1, Z):
+        src = gathered.at[0, c, y, x]
+        pending["z", Z - step] = send(src, gathered.at[Z - step, c, y, x], place(y, planes[step], x, c))
+
+    def gather_first(j):
+        if j:
+            pending["z", j].wait_recv()
+        for name, cols, device in (("fa", first_cols, by_x), ("fb", second_cols, by_y)):
+            ref = gathered.at[j, c, y, x, :, cols]
+            pending[name, j] = send(ref, ref, device)
+
+    def gather_second(j):
+        pending["fa", j].wait_recv()
+        ref = gathered.at[j, c, y, :, :, first_cols]
+        pending["sa", j] = send(ref, ref, by_y)
+        pending["fb", j].wait_recv()
+        ref = gathered.at[j, c, :, x, :, second_cols]
+        pending["sb", j] = send(ref, ref, by_x)
+
+    def gather_core(j):
+        pending["sa", j].wait_recv()
+        pending["sb", j].wait_recv()
+        ref = gathered.at[j, c]
+        pending["c", j] = send(ref, ref, by_c)
+
+    def evaluate(j):
+        pending["c", j].wait_recv()
+        if j == 0:
+            for load in loads:
+                load.wait()
+        group = C * Y * X * rows
+        features = gathered[j, :, :, :, :, LANES:near].reshape(group, width)
+        row_grads = gathered[j, :, :, :, :, near:].reshape(group, width)
+        extra = gathered[j, :, :, :, :, :LANES].reshape(group, LANES).astype(jnp.float32)
+        lanes = lax.broadcasted_iota(jnp.int32, (group, LANES), 1)
+        mine = lanes == expert
+        weight = jnp.sum(jnp.where(mine | (lanes == expert + experts), extra, 0.0), 1, keepdims=True)
+        contract = (((1,), (1,)), ((), ()))
+        pre_act = lax.dot_general(features, up[...], contract, preferred_element_type=jnp.float32)
+        gating = jax.nn.sigmoid(pre_act)
+        hidden = (pre_act * gating).astype(jnp.bfloat16)
+        hidden_grad = lax.dot_general(row_grads, down[...], contract, preferred_element_type=jnp.float32)
+        act_grad = (hidden_grad * gating * (1.0 + pre_act * (1.0 - gating))).astype(jnp.bfloat16)
+        products = jnp.sum(hidden.astype(jnp.float32) * hidden_grad, 1, keepdims=True)
+        partial[j, :, :, :, :, :LANES] = (
+            jnp.where(mine, products, 0.0).astype(jnp.bfloat16).reshape(C, Y, X, rows, LANES)
+        )
+        tile = min(512, width)
+        for left, matrix, base in ((hidden, down, LANES), (act_grad, up, near)):
+            for at in range(0, width, tile):
+                result = jnp.dot(left, matrix[:, at : at + tile], preferred_element_type=jnp.float32)
+                partial[j, :, :, :, :, base + at : base + at + tile] = (
+                    (result * weight).astype(jnp.bfloat16).reshape(C, Y, X, rows, tile)
+                )
+        pending["rc", j] = send(partial.at[j, far_c], from_core.at[j], by_c)
+
+    def add(one, other):
+        return (one.astype(jnp.float32) + other.astype(jnp.float32)).astype(jnp.bfloat16)
+
+    def reduce_first(j):
+        pending["rc", j].wait_recv()
+        core_sum[j] = add(partial[j, c], from_core[j])
+        pending["ra", j] = send(
+            core_sum.at[j, far_y, :, :, first_cols], from_first.at[j, :, :, first_cols], by_y
+        )
+        pending["rb", j] = send(
+            core_sum.at[j, :, far_x, :, second_cols], from_first.at[j, :, :, second_cols], by_x
+        )
+
+    def reduce_second(j):
+        pending["ra", j].wait_recv()
+        first_sum[j, :, :, :near] = add(core_sum[j, y, :, :, :near], from_first[j, :, :, :near])
+        pending["sra", j] = send(
+            first_sum.at[j, far_x, :, first_cols], from_second.at[j, :, first_cols], by_x
+        )
+        pending["rb", j].wait_recv()
+        for yy in range(Y):
+            first_sum[j, yy, :, near:] = add(core_sum[j, yy, x, :, near:], from_first[j, yy, :, near:])
+        pending["srb", j] = send(
+            first_sum.at[j, far_y, :, second_cols], from_second.at[j, :, second_cols], by_y
+        )
+
+    def reduce_plane(j):
+        pending["sra", j].wait_recv()
+        pending["srb", j].wait_recv()
+        plane_sum[j, :, :near] = add(first_sum[j, x, :, :near], from_second[j, :, :near])
+        plane_sum[j, :, near:] = add(first_sum[j, y, :, near:], from_second[j, :, near:])
+        if j:
+            pending["rz", j] = send(plane_sum.at[j], from_z.at[j], place(y, planes[j], x, c))
+
+    stages = (
+        gather_first, gather_second, gather_core, evaluate, reduce_first, reduce_second, reduce_plane
+    )
+    for slot in range(len(stages) + Z - 1):
+        for j in range(Z):
+            if 0 <= slot - j < len(stages):
+                stages[slot - j](j)
+
+    total = plane_sum[0].astype(jnp.float32)
+    for j in range(1, Z):
+        pending["rz", j].wait_recv()
+        total += from_z[j].astype(jnp.float32)
+    mixture_ref[...] = total[:, LANES:near].astype(jnp.bfloat16)
+    input_grad_ref[...] = total[:, near:].astype(jnp.bfloat16)
+    per_expert = total[:, :LANES]
+    slots = gate_ref.shape[1]
+    column = lax.broadcasted_iota(jnp.int32, (rows, slots), 1)
+    gate_grad = jnp.zeros((rows, slots), jnp.float32)
+    for k in range(slots):
+        value = jnp.sum(jnp.where(lane == ids_ref[:, k : k + 1], per_expert, 0.0), 1, keepdims=True)
+        gate_grad += jnp.where(column == k, value, 0.0)
+    gate_grad_ref[...] = gate_grad
+    for copy in started:
+        copy.wait_send()
+
+
+def token_shards(tokens, cotangent, gate_probs, expert_ids, up_weight, down_weight):
+    rows, width = tokens.shape
+    experts = lax.axis_size("expert")
+    hidden_part = up_weight.shape[1]
+    wide = LANES + 2 * width
+    kind = jnp.bfloat16
+    copies = 2 * (Z - 1) + 11 * Z
+    vmem = pl.BlockSpec(memory_space=pltpu.VMEM)
+    hbm = pl.BlockSpec(memory_space=pl.ANY)
+    return tuple(pl.pallas_call(
+        functools.partial(exchange_kernel, experts),
+        out_shape=(
+            jax.ShapeDtypeStruct((rows, width), kind),
+            jax.ShapeDtypeStruct((rows, width), kind),
+            jax.ShapeDtypeStruct(gate_probs.shape, jnp.float32),
+        ),
+        in_specs=[vmem, vmem, vmem, vmem, hbm, hbm],
+        out_specs=(vmem, vmem, vmem),
+        scratch_shapes=[
+            pltpu.VMEM((hidden_part, width), kind),
+            pltpu.VMEM((hidden_part, width), kind),
+            pltpu.VMEM((Z, C, Y, X, rows, wide), kind),
+            pltpu.VMEM((Z, C, Y, X, rows, wide), kind),
+            pltpu.VMEM((Z, Y, X, rows, wide), kind),
+            pltpu.VMEM((Z, Y, X, rows, wide), kind),
+            pltpu.VMEM((Z, 2, rows, wide), kind),
+            pltpu.VMEM((Z, 2, rows, wide), kind),
+            pltpu.VMEM((Z, rows, wide), kind),
+            pltpu.VMEM((Z, rows, wide), kind),
+            pltpu.VMEM((Z, rows, wide), kind),
+            pltpu.SemaphoreType.DMA((2,)),
+            pltpu.SemaphoreType.DMA((copies,)),
+            pltpu.SemaphoreType.DMA((copies,)),
+        ],
+        compiler_params=pltpu.CompilerParams(
+            collective_id=0, has_side_effects=True, vmem_limit_bytes=48 * 1024 * 1024
+        ),
+    )(tokens, cotangent, gate_probs, expert_ids, up_weight, down_weight))
+
+
 def solution(mesh):
+    small = dict(mesh.shape) == {"dp": Y, "expert": Z * X * C}
     placed = (
         P(("dp", "expert"), None),
         P(("dp", "expert"), None),
@@ -97,7 +329,7 @@
         P("expert", "dp", None),
     )
     return jax.shard_map(
-        shards,
+        token_shards if small else shards,
         mesh=mesh,
         in_specs=placed,
         out_specs=(P(("dp", "expert"), None), P(("dp", "expert"), None), P(("dp", "expert"), None)),

time: 229 us -> 70.7 us (0.31)
  waiting for transfers between devices: 166 us -> 0 us
  Pallas kernels: 0 us -> 61.8 us
  matrix products: 19.7 us -> 0 us
  between operations: 16.6 us -> 0.64 us
  starting transfers between devices: 10.8 us -> 0 us
  other arithmetic: 8.34 us -> 0 us
    psum x1 -> x0, waiting for transfers between devices: 103 us -> none  [broadcast(): return lax.psum(block, axis)]
    pallas_call x0 -> x1, Pallas kernels: none -> 61.8 us  [token_shards(): pl.pallas_call(functools.partial(exchange_kernel, experts), out_shape=(ja...]
    all_gather x4 -> x0, waiting for transfers between devices: 38.9 us -> none  [the longest x2 38.9 us: spread(): down_piece = lax.all_gather(down_parts, 'dp', axis=1, tiled=True)]
    all_to_all x2 -> x0, waiting for transfers between devices: 22.2 us -> none  [the longest x1 22.2 us: shards(): lax.all_to_all(outgoing, 'expert', split_axis=0, concat_axis=0, tiled=True)]
    dot_general x6 -> x0, matrix products: 19.7 us -> none  [the longest x2 8.94 us: expert_terms(): input_rows = jnp.dot(act_grad, up_piece, preferred_element_type=jnp.float32)]
    all_to_all x2 -> x0, starting transfers between devices: 10.6 us -> none  [the longest x1 6.9 us: shards(): lax.all_to_all(returning, 'expert', split_axis=0, concat_axis=0, tiled=True)]
    unnamed x19 -> x12, local copies, waits for them, and re-layouts: 2.34 us -> 7.27 us
    select_n x4 -> x0, other arithmetic: 2.54 us -> none  [the longest x2 2.52 us: broadcast(): jnp.where(lax.axis_index(axis) == owner, block, jnp.zeros_like(block))]
  transfers between devices with their start and end apart: 7 -> 0, of which waited for: 3 -> 0; matrix products, arithmetic and copies ran while one was open for 11% -> 0% of each run, Pallas kernels for 0% -> 0%
where the time goes in v1:
time: 70.7 us; the launch traced here: 70.4 us
  Pallas kernels  61.8 us (87%)
  local copies, waits for them, and re-layouts  7.93 us (11%)
    pallas_call x1, Pallas kernels, token_shards(): pl.pallas_call(functools.partial(exchange_kernel, experts), out_shape=(ja...  61.8 us
    unnamed x12, local copies, waits for them, and re-layouts  7.27 us

profile of v1, /device:TPU:0, one launch (start us, length us, event | category | flops | bytes accessed | tf_op | source)
XLA Modules:
  0.0 70.4 jit_solution(6527146855907982002)
XLA Ops:
  0.6 0.8 %copy.9.gate_ref = f32[16,8]{1,0:T(8,128)S(1)} copy(f32[16,8]{0,1:T(8,128)} %param.8) | data formatting | bytes 1024 | tf_op args[2]
  1.4 0.8 %copy.10.ids_ref = s32[16,8]{1,0:T(8,128)S(1)} copy(s32[16,8]{0,1:T(8,128)} %param.9) | data formatting | bytes 1024 | tf_op args[3]
  2.1 0.0 copy-start
  2.1 1.4 %copy-done = bf16[1,384,2048]{2,1,0:T(8,128)(2,1)S(1)} copy-done((bf16[1,384,2048]{2,1,0:T(8,128)(2,1)S(1)}, bf16[1,384,2048]{2,1,0:T(8,128)(2,1)}, u32[]{:S(2)}) %copy-start) | copy-done | bytes 1572888
  3.6 0.0 copy-start.1
  3.6 1.4 %copy-done.1 = bf16[1,384,2048]{2,1,0:T(8,128)(2,1)S(1)} copy-done((bf16[1,384,2048]{2,1,0:T(8,128)(2,1)S(1)}, bf16[1,384,2048]{2,1,0:T(8,128)(2,1)}, u32[]{:S(2)}) %copy-start.1) | copy-done | bytes 1572888
  5.0 0.0 copy-start.2
  5.0 0.8 %copy-done.2 = bf16[16,2048]{1,0:T(8,128)(2,1)S(1)} copy-done((bf16[16,2048]{1,0:T(8,128)(2,1)S(1)}, bf16[16,2048]{1,0:T(8,128)(2,1)}, u32[]{:S(2)}) %copy-start.2) | copy-done | bytes 65560
  5.8 0.0 copy-start.3
  5.8 0.8 %copy-done.3 = bf16[16,2048]{1,0:T(8,128)(2,1)S(1)} copy-done((bf16[16,2048]{1,0:T(8,128)(2,1)S(1)}, bf16[16,2048]{1,0:T(8,128)(2,1)}, u32[]{:S(2)}) %copy-start.3) | copy-done | bytes 65560
  6.6 61.8 %shard_map.85 = (bf16[16,2048]{1,0:T(8,128)(2,1)S(1)}, bf16[16,2048]{1,0:T(8,128)(2,1)S(1)}, f32[16,8]{1,0:T(8,128)S(1)}) custom-call(bf16[16,2048]{1,0:T(8,128)(2,1)S(1)} %copy-done.2, bf16[16,2048]{1,0:T(8,128)(2,1)S(1)} %copy-done.3, f32[16,8]{1,0:T(8,128)S(1)} %copy.9.gate_ref, s32[16,8]{1,0:T(8,128)S(1)} %copy.10.ids_ref, ...), custom_call_target="tpu_custom_call" | custom-call | tf_op jit(solution)/shard_map/pallas_call | solution.py:290
  68.5 0.7 copy.11
  69.1 0.6 copy.14
  69.8 0.6 copy.15
Async XLA Ops:
  2.1 1.4 %copy-start = (bf16[1,384,2048]{2,1,0:T(8,128)(2,1)S(1)}, bf16[1,384,2048]{2,1,0:T(8,128)(2,1)}, u32[]{:S(2)}) copy-start(bf16[1,384,2048]{2,1,0:T(8,128)(2,1)} %up_hbm.1) | copy-start | bytes 4718596
  3.6 1.4 %copy-start.1 = (bf16[1,384,2048]{2,1,0:T(8,128)(2,1)S(1)}, bf16[1,384,2048]{2,1,0:T(8,128)(2,1)}, u32[]{:S(2)}) copy-start(bf16[1,384,2048]{2,1,0:T(8,128)(2,1)} %down_hbm.1) | copy-start | bytes 4718596
  5.0 0.8 %copy-start.2 = (bf16[16,2048]{1,0:T(8,128)(2,1)S(1)}, bf16[16,2048]{1,0:T(8,128)(2,1)}, u32[]{:S(2)}) copy-start(bf16[16,2048]{1,0:T(8,128)(2,1)} %tokens_ref.1) | copy-start | bytes 196612
  5.8 0.8 %copy-start.3 = (bf16[16,2048]{1,0:T(8,128)(2,1)S(1)}, bf16[16,2048]{1,0:T(8,128)(2,1)}, u32[]{:S(2)}) copy-start(bf16[16,2048]{1,0:T(8,128)(2,1)} %cotangent_ref.1) | copy-start | bytes 196612

commit v2 on v1

--- a/solution.py
+++ b/solution.py
@@ -98,14 +98,14 @@
 
 def exchange_kernel(
     experts,
-    tokens_ref, cotangent_ref, gate_ref, ids_ref, up_hbm, down_hbm,
+    tokens_hbm, cotangent_hbm, gate_ref, ids_ref, up_hbm, down_hbm,
     mixture_ref, input_grad_ref, gate_grad_ref,
     up, down, gathered, partial, from_core, core_sum, from_first, first_sum, from_second, plane_sum, from_z,
     load_sem, send_sem, recv_sem,
 ):
-    width = tokens_ref.shape[1]
+    width = tokens_hbm.shape[1]
     near = LANES + width
-    rows = tokens_ref.shape[0]
+    rows = tokens_hbm.shape[0]
     y, expert = lax.axis_index("dp"), lax.axis_index("expert")
     z = expert // (X * C)
     x = (expert // C) % X
@@ -116,11 +116,13 @@
         return (yy, (zz * X + xx) * C + cc)
 
     by_x, by_y, by_c = place(y, z, far_x, c), place(far_y, z, x, c), place(y, z, x, far_c)
-    planes = [(z + step) % Z for step in range(Z)]
+    planes = [z, z + 1 - 2 * (z % 2), (z + 2) % Z, Z - 1 - z]
 
     loads = [
-        pltpu.make_async_copy(up_hbm.at[0], up, load_sem.at[0]),
-        pltpu.make_async_copy(down_hbm.at[0], down, load_sem.at[1]),
+        pltpu.make_async_copy(tokens_hbm, gathered.at[0, c, y, x, :, pl.ds(LANES, width)], load_sem.at[0]),
+        pltpu.make_async_copy(cotangent_hbm, gathered.at[0, c, y, x, :, pl.ds(near, width)], load_sem.at[1]),
+        pltpu.make_async_copy(up_hbm.at[0], up, load_sem.at[2]),
+        pltpu.make_async_copy(down_hbm.at[0], down, load_sem.at[3]),
     ]
     for load in loads:
         load.start()
@@ -130,22 +132,23 @@
     for partner in partners:
         pl.semaphore_signal(barrier, inc=1, device_id=partner, device_id_type=MESH)
 
-    lane = lax.broadcasted_iota(jnp.int32, (rows, LANES), 1)
-    weights = jnp.zeros((rows, LANES), jnp.float32)
-    for k in range(gate_ref.shape[1]):
-        weights += jnp.where(lane == ids_ref[:, k : k + 1], gate_ref[:, k : k + 1], 0.0)
-    high = weights.astype(jnp.bfloat16).astype(jnp.float32)
-    rest = jnp.zeros((rows, LANES), jnp.float32)
-    for k in range(gate_ref.shape[1]):
-        gate = gate_ref[:, k : k + 1]
-        rest += jnp.where(
-            lane == ids_ref[:, k : k + 1] + experts,
-            gate - gate.astype(jnp.bfloat16).astype(jnp.float32),
-            0.0,
-        )
-    gathered[0, c, y, x, :, :LANES] = (high + rest).astype(jnp.bfloat16)
-    gathered[0, c, y, x, :, LANES:near] = tokens_ref[...]
-    gathered[0, c, y, x, :, near:] = cotangent_ref[...]
+    slots = gate_ref.shape[0]
+    names = lax.broadcasted_iota(jnp.int32, (LANES, rows), 0)
+    weights = jnp.zeros((LANES, rows), jnp.float32)
+    for k in range(slots):
+        gate, chosen = gate_ref[k : k + 1, :], ids_ref[k : k + 1, :]
+        high = gate.astype(jnp.bfloat16).astype(jnp.float32)
+        weights += jnp.where(names == chosen, high, 0.0)
+        weights += jnp.where(names == chosen + experts, gate - high, 0.0)
+    square = (rows, rows)
+    diagonal = lax.broadcasted_iota(jnp.int32, square, 0) == lax.broadcasted_iota(jnp.int32, square, 1)
+    turned = lax.dot_general(
+        jnp.where(diagonal, 1.0, 0.0).astype(jnp.bfloat16), weights.astype(jnp.bfloat16),
+        (((1,), (1,)), ((), ())), preferred_element_type=jnp.float32,
+    )
+    gathered[0, c, y, x, :, :LANES] = turned.astype(jnp.bfloat16)
+    loads[0].wait()
+    loads[1].wait()
     pl.semaphore_wait(barrier, len(partners))
 
     started = []
@@ -162,9 +165,10 @@
 
     first_cols, second_cols = pl.ds(0, near), pl.ds(near, width)
     pending = {}
-    for step in range(1, Z):
+
+    def send_plane(j):
         src = gathered.at[0, c, y, x]
-        pending["z", Z - step] = send(src, gathered.at[Z - step, c, y, x], place(y, planes[step], x, c))
+        pending["z", j] = send(src, gathered.at[j, c, y, x], place(y, planes[j], x, c))
 
     def gather_first(j):
         if j:
@@ -190,8 +194,8 @@
     def evaluate(j):
         pending["c", j].wait_recv()
         if j == 0:
-            for load in loads:
-                load.wait()
+            loads[2].wait()
+            loads[3].wait()
         group = C * Y * X * rows
         features = gathered[j, :, :, :, :, LANES:near].reshape(group, width)
         row_grads = gathered[j, :, :, :, :, near:].reshape(group, width)
@@ -252,13 +256,18 @@
         if j:
             pending["rz", j] = send(plane_sum.at[j], from_z.at[j], place(y, planes[j], x, c))
 
-    stages = (
-        gather_first, gather_second, gather_core, evaluate, reduce_first, reduce_second, reduce_plane
-    )
-    for slot in range(len(stages) + Z - 1):
-        for j in range(Z):
-            if 0 <= slot - j < len(stages):
-                stages[slot - j](j)
+    order = (
+        (send_plane, 1), (gather_first, 0), (send_plane, 2),
+        (gather_second, 0), (gather_first, 1), (send_plane, 3), (gather_core, 0),
+        (gather_second, 1), (gather_first, 2), (evaluate, 0),
+        (gather_core, 1), (gather_second, 2), (gather_first, 3), (evaluate, 1),
+        (gather_core, 2), (gather_second, 3), (reduce_first, 1), (evaluate, 2),
+        (gather_core, 3), (reduce_second, 1), (reduce_first, 2), (evaluate, 3),
+        (reduce_first, 0), (reduce_plane, 1), (reduce_second, 2), (reduce_first, 3),
+        (reduce_second, 0), (reduce_plane, 2), (reduce_second, 3), (reduce_plane, 3), (reduce_plane, 0),
+    )
+    for stage, j in order:
+        stage(j)
 
     total = plane_sum[0].astype(jnp.float32)
     for j in range(1, Z):
@@ -266,14 +275,14 @@
         total += from_z[j].astype(jnp.float32)
     mixture_ref[...] = total[:, LANES:near].astype(jnp.bfloat16)
     input_grad_ref[...] = total[:, near:].astype(jnp.bfloat16)
-    per_expert = total[:, :LANES]
-    slots = gate_ref.shape[1]
-    column = lax.broadcasted_iota(jnp.int32, (rows, slots), 1)
-    gate_grad = jnp.zeros((rows, slots), jnp.float32)
+    per_expert = lax.dot_general(
+        total[:, :LANES], jnp.where(diagonal, 1.0, 0.0), (((0,), (0,)), ((), ())),
+        precision=lax.Precision.HIGHEST, preferred_element_type=jnp.float32,
+    )
     for k in range(slots):
-        value = jnp.sum(jnp.where(lane == ids_ref[:, k : k + 1], per_expert, 0.0), 1, keepdims=True)
-        gate_grad += jnp.where(column == k, value, 0.0)
-    gate_grad_ref[...] = gate_grad
+        gate_grad_ref[k : k + 1, :] = jnp.sum(
+            jnp.where(names == ids_ref[k : k + 1, :], per_expert, 0.0), 0, keepdims=True
+        )
     for copy in started:
         copy.wait_send()
 
@@ -287,14 +296,14 @@
     copies = 2 * (Z - 1) + 11 * Z
     vmem = pl.BlockSpec(memory_space=pltpu.VMEM)
     hbm = pl.BlockSpec(memory_space=pl.ANY)
-    return tuple(pl.pallas_call(
+    mixture, input_grad, gate_grad = pl.pallas_call(
         functools.partial(exchange_kernel, experts),
         out_shape=(
             jax.ShapeDtypeStruct((rows, width), kind),
             jax.ShapeDtypeStruct((rows, width), kind),
-            jax.ShapeDtypeStruct(gate_probs.shape, jnp.float32),
+            jax.ShapeDtypeStruct(gate_probs.shape[::-1], jnp.float32),
         ),
-        in_specs=[vmem, vmem, vmem, vmem, hbm, hbm],
+        in_specs=[hbm, hbm, vmem, vmem, hbm, hbm],
         out_specs=(vmem, vmem, vmem),
         scratch_shapes=[
             pltpu.VMEM((hidden_part, width), kind),
@@ -308,14 +317,15 @@
             pltpu.VMEM((Z, rows, wide), kind),
             pltpu.VMEM((Z, rows, wide), kind),
             pltpu.VMEM((Z, rows, wide), kind),
-            pltpu.SemaphoreType.DMA((2,)),
+            pltpu.SemaphoreType.DMA((4,)),
             pltpu.SemaphoreType.DMA((copies,)),
             pltpu.SemaphoreType.DMA((copies,)),
         ],
         compiler_params=pltpu.CompilerParams(
-            collective_id=0, has_side_effects=True, vmem_limit_bytes=48 * 1024 * 1024
+            collective_id=0, has_side_effects=True, vmem_limit_bytes=60 * 1024 * 1024
         ),
-    )(tokens, cotangent, gate_probs, expert_ids, up_weight, down_weight))
+    )(tokens, cotangent, gate_probs.T, expert_ids.T, up_weight, down_weight)
+    return mixture, input_grad, gate_grad.T
 
 
 def solution(mesh):

time: 70.7 us -> 62 us (0.88)
  Pallas kernels: 61.8 us -> 56.9 us
  local copies, waits for them, and re-layouts: 7.93 us -> 4.22 us
    pallas_call x1, Pallas kernels: 61.8 us -> 56.9 us  [token_shards(): pl.pallas_call(functools.partial(exchange_kernel, experts), out_shape=(ja...]
    unnamed x12 -> x3, local copies, waits for them, and re-layouts: 7.27 us -> 4.22 us
where the time goes in v2:
time: 62 us; the launch traced here: 61.7 us
  Pallas kernels  56.9 us (92%)
  local copies, waits for them, and re-layouts  4.22 us (7%)
  between operations  0.64 us (1%)
    pallas_call x1, Pallas kernels, token_shards(): pl.pallas_call(functools.partial(exchange_kernel, experts), out_shape=(ja...  56.9 us
    unnamed x3, local copies, waits for them, and re-layouts  4.22 us

profile of v2, /device:TPU:0, one launch (start us, length us, event | category | flops | bytes accessed | tf_op | source)
XLA Modules:
  0.0 61.7 jit_solution(9573119308926958205)
XLA Ops:
  0.6 56.9 %shard_map.85 = (bf16[16,2048]{1,0:T(8,128)(2,1)}, bf16[16,2048]{1,0:T(8,128)(2,1)}, f32[8,16]{1,0:T(8,128)}) custom-call(bf16[16,2048]{1,0:T(8,128)(2,1)} %tokens_hbm.1, bf16[16,2048]{1,0:T(8,128)(2,1)} %cotangent_hbm.1, f32[8,16]{1,0:T(8,128)} %bitcast.3, s32[8,16]{1,0:T(8,128)} %bitcast.4, bf16[1,384,2048]{2,1,0:T(8,128)(2,1)} %up_hbm.1, ...), custom_call_target="tpu_custom_call" | custom-call | tf_op jit(solution)/shard_map/pallas_call | solution.py:299
  57.5 1.5 %copy.12 = bf16[16,2048]{1,0:T(8,128)(2,1)} copy(bf16[16,2048]{1,0:T(8,128)(2,1)} %get-tuple-element.12) | data formatting | bytes 131072
  59.0 1.5 %copy.13 = bf16[16,2048]{1,0:T(8,128)(2,1)} copy(bf16[16,2048]{1,0:T(8,128)(2,1)} %get-tuple-element.13) | data formatting | bytes 131072
  60.5 1.3 %copy.14 = f32[16,8]{0,1:T(8,128)} copy(f32[16,8]{0,1:T(8,128)} %bitcast.5) | data formatting | bytes 1024

commit v3 on v2

--- a/solution.py
+++ b/solution.py
@@ -116,7 +116,8 @@
         return (yy, (zz * X + xx) * C + cc)
 
     by_x, by_y, by_c = place(y, z, far_x, c), place(far_y, z, x, c), place(y, z, x, far_c)
-    planes = [z, z + 1 - 2 * (z % 2), (z + 2) % Z, Z - 1 - z]
+    planes = [z, z + 1 - 2 * (z % 2), Z - 1 - z, (z + 2) % Z]
+    inner = z % (Z - 1) > 0
 
     loads = [
         pltpu.make_async_copy(tokens_hbm, gathered.at[0, c, y, x, :, pl.ds(LANES, width)], load_sem.at[0]),
@@ -153,22 +154,40 @@
 
     started = []
 
-    def send(src, dst, device):
+    def prepare(src, dst, device):
         index = len(started)
         copy = pltpu.make_async_remote_copy(
             src_ref=src, dst_ref=dst, send_sem=send_sem.at[index], recv_sem=recv_sem.at[index],
             device_id=device, device_id_type=MESH,
         )
-        copy.start()
         started.append(copy)
         return copy
 
+    def send(src, dst, device):
+        copy = prepare(src, dst, device)
+        copy.start()
+        return copy
+
     first_cols, second_cols = pl.ds(0, near), pl.ds(near, width)
     pending = {}
 
+    for j in range(1, Z):
+        pending["z", j] = prepare(
+            gathered.at[0, c, y, x], gathered.at[j, c, y, x], place(y, planes[j], x, c)
+        )
+
     def send_plane(j):
-        src = gathered.at[0, c, y, x]
-        pending["z", j] = send(src, gathered.at[j, c, y, x], place(y, planes[j], x, c))
+        pending["z", j].start()
+
+    def send_inner(j):
+        @pl.when(inner)
+        def _():
+            pending["z", j].start()
+
+    def send_outer(j):
+        @pl.when(jnp.logical_not(inner))
+        def _():
+            pending["z", j].start()
 
     def gather_first(j):
         if j:
@@ -257,14 +276,13 @@
             pending["rz", j] = send(plane_sum.at[j], from_z.at[j], place(y, planes[j], x, c))
 
     order = (
-        (send_plane, 1), (gather_first, 0), (send_plane, 2),
-        (gather_second, 0), (gather_first, 1), (send_plane, 3), (gather_core, 0),
-        (gather_second, 1), (gather_first, 2), (evaluate, 0),
-        (gather_core, 1), (gather_second, 2), (gather_first, 3), (evaluate, 1),
+        (send_plane, 1), (send_inner, 2), (gather_first, 0), (gather_second, 0), (send_outer, 2),
+        (gather_first, 1), (send_plane, 3), (gather_core, 0), (gather_first, 2), (gather_second, 1),
+        (evaluate, 0), (gather_second, 2), (gather_core, 1), (gather_first, 3), (evaluate, 1),
         (gather_core, 2), (gather_second, 3), (reduce_first, 1), (evaluate, 2),
-        (gather_core, 3), (reduce_second, 1), (reduce_first, 2), (evaluate, 3),
-        (reduce_first, 0), (reduce_plane, 1), (reduce_second, 2), (reduce_first, 3),
-        (reduce_second, 0), (reduce_plane, 2), (reduce_second, 3), (reduce_plane, 3), (reduce_plane, 0),
+        (gather_core, 3), (reduce_first, 2), (evaluate, 3), (reduce_second, 1),
+        (reduce_first, 3), (reduce_second, 2), (reduce_plane, 1), (reduce_second, 3), (reduce_first, 0),
+        (reduce_plane, 2), (reduce_plane, 3), (reduce_second, 0), (reduce_plane, 0),
     )
     for stage, j in order:
         stage(j)

time: 62 us -> 61.5 us (level)
  no operation moved by 1% of the time
where the time goes in v3:
time: 61.5 us; the launch traced here: 61.2 us
  Pallas kernels  56.4 us (92%)
  local copies, waits for them, and re-layouts  4.22 us (7%)
  between operations  0.64 us (1%)
    pallas_call x1, Pallas kernels, token_shards(): pl.pallas_call(functools.partial(exchange_kernel, experts), out_shape=(ja...  56.4 us
    unnamed x3, local copies, waits for them, and re-layouts  4.22 us

profile of v3, /device:TPU:0, one launch (start us, length us, event | category | flops | bytes accessed | tf_op | source)
XLA Modules:
  0.0 61.2 jit_solution(9660723268126464866)
XLA Ops:
  0.6 56.4 %shard_map.85 = (bf16[16,2048]{1,0:T(8,128)(2,1)}, bf16[16,2048]{1,0:T(8,128)(2,1)}, f32[8,16]{1,0:T(8,128)}) custom-call(bf16[16,2048]{1,0:T(8,128)(2,1)} %tokens_hbm.1, bf16[16,2048]{1,0:T(8,128)(2,1)} %cotangent_hbm.1, f32[8,16]{1,0:T(8,128)} %bitcast.3, s32[8,16]{1,0:T(8,128)} %bitcast.4, bf16[1,384,2048]{2,1,0:T(8,128)(2,1)} %up_hbm.1, ...), custom_call_target="tpu_custom_call" | custom-call | tf_op jit(solution)/shard_map/pallas_call | solution.py:317
  57.0 1.5 %copy.12 = bf16[16,2048]{1,0:T(8,128)(2,1)} copy(bf16[16,2048]{1,0:T(8,128)(2,1)} %get-tuple-element.12) | data formatting | bytes 131072
  58.5 1.5 %copy.13 = bf16[16,2048]{1,0:T(8,128)(2,1)} copy(bf16[16,2048]{1,0:T(8,128)(2,1)} %get-tuple-element.13) | data formatting | bytes 131072
  59.9 1.3 %copy.14 = f32[16,8]{0,1:T(8,128)} copy(f32[16,8]{0,1:T(8,128)} %bitcast.5) | data formatting | bytes 1024

commit v4 on v3

--- a/solution.py
+++ b/solution.py
@@ -100,7 +100,7 @@
     experts,
     tokens_hbm, cotangent_hbm, gate_ref, ids_ref, up_hbm, down_hbm,
     mixture_ref, input_grad_ref, gate_grad_ref,
-    up, down, gathered, partial, from_core, core_sum, from_first, first_sum, from_second, plane_sum, from_z,
+    up, down, up_turned, down_turned, gathered, partial, from_core, core_sum, from_first, first_sum, from_second, plane_sum, from_z,
     load_sem, send_sem, recv_sem,
 ):
     width = tokens_hbm.shape[1]
@@ -210,11 +210,15 @@
         ref = gathered.at[j, c]
         pending["c", j] = send(ref, ref, by_c)
 
+    def turn(index):
+        loads[2 + index].wait()
+        matrix, turned = ((up, up_turned), (down, down_turned))[index]
+        block = min(256, width)
+        for at in range(0, width, block):
+            turned[at : at + block, :] = matrix[:, at : at + block].T
+
     def evaluate(j):
         pending["c", j].wait_recv()
-        if j == 0:
-            loads[2].wait()
-            loads[3].wait()
         group = C * Y * X * rows
         features = gathered[j, :, :, :, :, LANES:near].reshape(group, width)
         row_grads = gathered[j, :, :, :, :, near:].reshape(group, width)
@@ -222,11 +226,10 @@
         lanes = lax.broadcasted_iota(jnp.int32, (group, LANES), 1)
         mine = lanes == expert
         weight = jnp.sum(jnp.where(mine | (lanes == expert + experts), extra, 0.0), 1, keepdims=True)
-        contract = (((1,), (1,)), ((), ()))
-        pre_act = lax.dot_general(features, up[...], contract, preferred_element_type=jnp.float32)
+        pre_act = jnp.dot(features, up_turned[...], preferred_element_type=jnp.float32)
         gating = jax.nn.sigmoid(pre_act)
         hidden = (pre_act * gating).astype(jnp.bfloat16)
-        hidden_grad = lax.dot_general(row_grads, down[...], contract, preferred_element_type=jnp.float32)
+        hidden_grad = jnp.dot(row_grads, down_turned[...], preferred_element_type=jnp.float32)
         act_grad = (hidden_grad * gating * (1.0 + pre_act * (1.0 - gating))).astype(jnp.bfloat16)
         products = jnp.sum(hidden.astype(jnp.float32) * hidden_grad, 1, keepdims=True)
         partial[j, :, :, :, :, :LANES] = (
@@ -276,7 +279,8 @@
             pending["rz", j] = send(plane_sum.at[j], from_z.at[j], place(y, planes[j], x, c))
 
     order = (
-        (send_plane, 1), (send_inner, 2), (gather_first, 0), (gather_second, 0), (send_outer, 2),
+        (send_plane, 1), (send_inner, 2), (gather_first, 0), (turn, 0), (gather_second, 0), (send_outer, 2),
+        (turn, 1),
         (gather_first, 1), (send_plane, 3), (gather_core, 0), (gather_first, 2), (gather_second, 1),
         (evaluate, 0), (gather_second, 2), (gather_core, 1), (gather_first, 3), (evaluate, 1),
         (gather_core, 2), (gather_second, 3), (reduce_first, 1), (evaluate, 2),
@@ -326,6 +330,8 @@
         scratch_shapes=[
             pltpu.VMEM((hidden_part, width), kind),
             pltpu.VMEM((hidden_part, width), kind),
+            pltpu.VMEM((width, hidden_part), kind),
+            pltpu.VMEM((width, hidden_part), kind),
             pltpu.VMEM((Z, C, Y, X, rows, wide), kind),
             pltpu.VMEM((Z, C, Y, X, rows, wide), kind),
             pltpu.VMEM((Z, Y, X, rows, wide), kind),
@@ -340,7 +346,7 @@
             pltpu.SemaphoreType.DMA((copies,)),
         ],
         compiler_params=pltpu.CompilerParams(
-            collective_id=0, has_side_effects=True, vmem_limit_bytes=60 * 1024 * 1024
+            collective_id=0, has_side_effects=True, vmem_limit_bytes=53500 * 1024
         ),
     )(tokens, cotangent, gate_probs.T, expert_ids.T, up_weight, down_weight)
     return mixture, input_grad, gate_grad.T

time: 61.5 us -> 60.3 us (0.980)
  Pallas kernels: 56.4 us -> 54.5 us
  local copies, waits for them, and re-layouts: 4.22 us -> 4.9 us
    pallas_call x1, Pallas kernels: 56.4 us -> 54.5 us  [token_shards(): pl.pallas_call(functools.partial(exchange_kernel, experts), out_shape=(ja...]
    unnamed x3 -> x11, local copies, waits for them, and re-layouts: 4.22 us -> 4.9 us
where the time goes in v4:
time: 60.3 us; the launch traced here: 60 us
  Pallas kernels  54.5 us (90%)
  local copies, waits for them, and re-layouts  4.9 us (8%)
  between operations  0.65 us (1%)
    pallas_call x1, Pallas kernels, token_shards(): pl.pallas_call(functools.partial(exchange_kernel, experts), out_shape=(ja...  54.5 us
    unnamed x11, local copies, waits for them, and re-layouts  4.9 us

profile of v4, /device:TPU:0, one launch (start us, length us, event | category | flops | bytes accessed | tf_op | source)
XLA Modules:
  0.0 60.0 jit_solution(17495033922049475803)
XLA Ops:
  0.6 0.0 copy-start
  0.6 0.8 %copy-done = bf16[16,2048]{1,0:T(8,128)(2,1)S(1)} copy-done((bf16[16,2048]{1,0:T(8,128)(2,1)S(1)}, bf16[16,2048]{1,0:T(8,128)(2,1)}, u32[]{:S(2)}) %copy-start) | copy-done | bytes 65560
  1.5 0.0 copy-start.1
  1.5 0.8 %copy-done.1 = bf16[16,2048]{1,0:T(8,128)(2,1)S(1)} copy-done((bf16[16,2048]{1,0:T(8,128)(2,1)S(1)}, bf16[16,2048]{1,0:T(8,128)(2,1)}, u32[]{:S(2)}) %copy-start.1) | copy-done | bytes 65560
  2.3 0.0 copy-start.2
  2.3 0.7 %copy-done.2 = f32[16,8]{0,1:T(8,128)S(1)} copy-done((f32[16,8]{0,1:T(8,128)S(1)}, f32[16,8]{0,1:T(8,128)}, u32[]{:S(2)}) %copy-start.2) | copy-done | bytes 536
  3.0 0.0 copy-start.3
  3.0 0.7 %copy-done.3 = s32[16,8]{0,1:T(8,128)S(1)} copy-done((s32[16,8]{0,1:T(8,128)S(1)}, s32[16,8]{0,1:T(8,128)}, u32[]{:S(2)}) %copy-start.3) | copy-done | bytes 536
  3.7 54.5 %shard_map.85 = (bf16[16,2048]{1,0:T(8,128)(2,1)S(1)}, bf16[16,2048]{1,0:T(8,128)(2,1)S(1)}, f32[8,16]{1,0:T(8,128)S(1)}) custom-call(bf16[16,2048]{1,0:T(8,128)(2,1)S(1)} %copy-done, bf16[16,2048]{1,0:T(8,128)(2,1)S(1)} %copy-done.1, f32[8,16]{1,0:T(8,128)S(1)} %bitcast.3, s32[8,16]{1,0:T(8,128)S(1)} %bitcast.4, bf16[1,384,2048]{2,1,0:T(8,128)(2,1)} %up_hbm.1, ...), custom_call_target="tpu_custom_call" | custom-call | tf_op jit(solution)/shard_map/pallas_call | solution.py:321
  58.2 0.6 %copy.12 = bf16[16,2048]{1,0:T(8,128)(2,1)} copy(bf16[16,2048]{1,0:T(8,128)(2,1)S(1)} %get-tuple-element.12) | data formatting | bytes 131072
  58.8 0.6 %copy.13 = bf16[16,2048]{1,0:T(8,128)(2,1)} copy(bf16[16,2048]{1,0:T(8,128)(2,1)S(1)} %get-tuple-element.13) | data formatting | bytes 131072
  59.4 0.6 copy.14
Async XLA Ops:
  0.6 0.8 %copy-start = (bf16[16,2048]{1,0:T(8,128)(2,1)S(1)}, bf16[16,2048]{1,0:T(8,128)(2,1)}, u32[]{:S(2)}) copy-start(bf16[16,2048]{1,0:T(8,128)(2,1)} %tokens_hbm.1) | copy-start | bytes 196612
  1.5 0.8 %copy-start.1 = (bf16[16,2048]{1,0:T(8,128)(2,1)S(1)}, bf16[16,2048]{1,0:T(8,128)(2,1)}, u32[]{:S(2)}) copy-start(bf16[16,2048]{1,0:T(8,128)(2,1)} %cotangent_hbm.1) | copy-start | bytes 196612
  2.3 0.7 %copy-start.2 = (f32[16,8]{0,1:T(8,128)S(1)}, f32[16,8]{0,1:T(8,128)}, u32[]{:S(2)}) copy-start(f32[16,8]{0,1:T(8,128)} %param.8) | copy-start | bytes 1540
  3.0 0.7 %copy-start.3 = (s32[16,8]{0,1:T(8,128)S(1)}, s32[16,8]{0,1:T(8,128)}, u32[]{:S(2)}) copy-start(s32[16,8]{0,1:T(8,128)} %param.9) | copy-start | bytes 1540

commit v5 on v4

--- a/solution.py
+++ b/solution.py
@@ -205,10 +205,10 @@
         pending["sb", j] = send(ref, ref, by_x)
 
     def gather_core(j):
-        pending["sa", j].wait_recv()
-        pending["sb", j].wait_recv()
-        ref = gathered.at[j, c]
-        pending["c", j] = send(ref, ref, by_c)
+        for name, cols in (("a", first_cols), ("b", second_cols)):
+            pending["s" + name, j].wait_recv()
+            ref = gathered.at[j, c, :, :, :, cols]
+            pending["c" + name, j] = send(ref, ref, by_c)
 
     def turn(index):
         loads[2 + index].wait()
@@ -218,10 +218,9 @@
             turned[at : at + block, :] = matrix[:, at : at + block].T
 
     def evaluate(j):
-        pending["c", j].wait_recv()
+        pending["ca", j].wait_recv()
         group = C * Y * X * rows
         features = gathered[j, :, :, :, :, LANES:near].reshape(group, width)
-        row_grads = gathered[j, :, :, :, :, near:].reshape(group, width)
         extra = gathered[j, :, :, :, :, :LANES].reshape(group, LANES).astype(jnp.float32)
         lanes = lax.broadcasted_iota(jnp.int32, (group, LANES), 1)
         mine = lanes == expert
@@ -229,6 +228,8 @@
         pre_act = jnp.dot(features, up_turned[...], preferred_element_type=jnp.float32)
         gating = jax.nn.sigmoid(pre_act)
         hidden = (pre_act * gating).astype(jnp.bfloat16)
+        pending["cb", j].wait_recv()
+        row_grads = gathered[j, :, :, :, :, near:].reshape(group, width)
         hidden_grad = jnp.dot(row_grads, down_turned[...], preferred_element_type=jnp.float32)
         act_grad = (hidden_grad * gating * (1.0 + pre_act * (1.0 - gating))).astype(jnp.bfloat16)
         products = jnp.sum(hidden.astype(jnp.float32) * hidden_grad, 1, keepdims=True)
@@ -236,23 +237,29 @@
             jnp.where(mine, products, 0.0).astype(jnp.bfloat16).reshape(C, Y, X, rows, LANES)
         )
         tile = min(512, width)
-        for left, matrix, base in ((hidden, down, LANES), (act_grad, up, near)):
+        for name, left, matrix, base, cols in (
+            ("rca", hidden, down, LANES, first_cols), ("rcb", act_grad, up, near, second_cols)
+        ):
             for at in range(0, width, tile):
                 result = jnp.dot(left, matrix[:, at : at + tile], preferred_element_type=jnp.float32)
                 partial[j, :, :, :, :, base + at : base + at + tile] = (
                     (result * weight).astype(jnp.bfloat16).reshape(C, Y, X, rows, tile)
                 )
-        pending["rc", j] = send(partial.at[j, far_c], from_core.at[j], by_c)
+            pending[name, j] = send(
+                partial.at[j, far_c, :, :, :, cols], from_core.at[j, :, :, :, cols], by_c
+            )
 
     def add(one, other):
         return (one.astype(jnp.float32) + other.astype(jnp.float32)).astype(jnp.bfloat16)
 
     def reduce_first(j):
-        pending["rc", j].wait_recv()
-        core_sum[j] = add(partial[j, c], from_core[j])
+        pending["rca", j].wait_recv()
+        core_sum[j, :, :, :, :near] = add(partial[j, c, :, :, :, :near], from_core[j, :, :, :, :near])
         pending["ra", j] = send(
             core_sum.at[j, far_y, :, :, first_cols], from_first.at[j, :, :, first_cols], by_y
         )
+        pending["rcb", j].wait_recv()
+        core_sum[j, :, :, :, near:] = add(partial[j, c, :, :, :, near:], from_core[j, :, :, :, near:])
         pending["rb", j] = send(
             core_sum.at[j, :, far_x, :, second_cols], from_first.at[j, :, :, second_cols], by_x
         )
@@ -271,12 +278,16 @@
         )
 
     def reduce_plane(j):
-        pending["sra", j].wait_recv()
-        pending["srb", j].wait_recv()
-        plane_sum[j, :, :near] = add(first_sum[j, x, :, :near], from_second[j, :, :near])
-        plane_sum[j, :, near:] = add(first_sum[j, y, :, near:], from_second[j, :, near:])
-        if j:
-            pending["rz", j] = send(plane_sum.at[j], from_z.at[j], place(y, planes[j], x, c))
+        for name, cols, kept in (
+            ("a", slice(0, near), x), ("b", slice(near, near + width), y)
+        ):
+            pending["sr" + name, j].wait_recv()
+            plane_sum[j, :, cols] = add(first_sum[j, kept, :, cols], from_second[j, :, cols])
+            if j:
+                part = first_cols if name == "a" else second_cols
+                pending["rz" + name, j] = send(
+                    plane_sum.at[j, :, part], from_z.at[j, :, part], place(y, planes[j], x, c)
+                )
 
     order = (
         (send_plane, 1), (send_inner, 2), (gather_first, 0), (turn, 0), (gather_second, 0), (send_outer, 2),
@@ -293,7 +304,8 @@
 
     total = plane_sum[0].astype(jnp.float32)
     for j in range(1, Z):
-        pending["rz", j].wait_recv()
+        pending["rza", j].wait_recv()
+        pending["rzb", j].wait_recv()
         total += from_z[j].astype(jnp.float32)
     mixture_ref[...] = total[:, LANES:near].astype(jnp.bfloat16)
     input_grad_ref[...] = total[:, near:].astype(jnp.bfloat16)
@@ -309,16 +321,26 @@
         copy.wait_send()
 
 
+def deliver_kernel(*refs):
+    sem = refs[-1]
+    half = (len(refs) - 1) // 2
+    copies = [pltpu.make_async_copy(refs[i], refs[half + i], sem.at[i]) for i in range(half)]
+    for copy in copies:
+        copy.start()
+    for copy in copies:
+        copy.wait()
+
+
 def token_shards(tokens, cotangent, gate_probs, expert_ids, up_weight, down_weight):
     rows, width = tokens.shape
     experts = lax.axis_size("expert")
     hidden_part = up_weight.shape[1]
     wide = LANES + 2 * width
     kind = jnp.bfloat16
-    copies = 2 * (Z - 1) + 11 * Z
+    copies = 15 * Z
     vmem = pl.BlockSpec(memory_space=pltpu.VMEM)
     hbm = pl.BlockSpec(memory_space=pl.ANY)
-    mixture, input_grad, gate_grad = pl.pallas_call(
+    results = pl.pallas_call(
         functools.partial(exchange_kernel, experts),
         out_shape=(
             jax.ShapeDtypeStruct((rows, width), kind),
@@ -346,9 +368,17 @@
             pltpu.SemaphoreType.DMA((copies,)),
         ],
         compiler_params=pltpu.CompilerParams(
-            collective_id=0, has_side_effects=True, vmem_limit_bytes=53500 * 1024
+            collective_id=0, has_side_effects=True, vmem_limit_bytes=60 * 1024 * 1024
         ),
     )(tokens, cotangent, gate_probs.T, expert_ids.T, up_weight, down_weight)
+    mixture, input_grad, gate_grad = pl.pallas_call(
+        deliver_kernel,
+        out_shape=tuple(jax.ShapeDtypeStruct(result.shape, result.dtype) for result in results),
+        in_specs=[hbm] * len(results),
+        out_specs=(hbm,) * len(results),
+        scratch_shapes=[pltpu.SemaphoreType.DMA((len(results),))],
+        compiler_params=pltpu.CompilerParams(vmem_limit_bytes=60 * 1024 * 1024),
+    )(*results)
     return mixture, input_grad, gate_grad.T
 
 

time: 60.3 us -> 61.8 us (1.025)
  Pallas kernels: 54.5 us -> 60.9 us
  local copies, waits for them, and re-layouts: 4.9 us -> 0 us
    pallas_call x0 -> x1, Pallas kernels: none -> 5.22 us  [token_shards(): pl.pallas_call(deliver_kernel, out_shape=tuple((jax.ShapeDtypeStruct(resu...]
    unnamed x11 -> x0, local copies, waits for them, and re-layouts: 4.9 us -> none
    pallas_call x1, Pallas kernels: 54.5 us -> 55.7 us  [token_shards(): pl.pallas_call(functools.partial(exchange_kernel, experts), out_shape=(ja...]
where the time goes in v5:
time: 61.8 us; the launch traced here: 61.5 us
  Pallas kernels  60.9 us (99%)
  between operations  0.64 us (1%)
    pallas_call x1, Pallas kernels, token_shards(): pl.pallas_call(functools.partial(exchange_kernel, experts), out_shape=(ja...  55.7 us
    pallas_call x1, Pallas kernels, token_shards(): pl.pallas_call(deliver_kernel, out_shape=tuple((jax.ShapeDtypeStruct(resu...  5.22 us

profile of v5, /device:TPU:0, one launch (start us, length us, event | category | flops | bytes accessed | tf_op | source)
XLA Modules:
  0.0 61.5 jit_solution(3933192937156600486)
XLA Ops:
  0.6 55.7 %shard_map.85 = (bf16[16,2048]{1,0:T(8,128)(2,1)}, bf16[16,2048]{1,0:T(8,128)(2,1)}, f32[8,16]{1,0:T(8,128)}) custom-call(bf16[16,2048]{1,0:T(8,128)(2,1)} %tokens_hbm.1, bf16[16,2048]{1,0:T(8,128)(2,1)} %cotangent_hbm.1, f32[8,16]{1,0:T(8,128)} %bitcast.3, s32[8,16]{1,0:T(8,128)} %bitcast.4, bf16[1,384,2048]{2,1,0:T(8,128)(2,1)} %up_hbm.1, ...), custom_call_target="tpu_custom_call" | custom-call | tf_op jit(solution)/shard_map/pallas_call | solution.py:343
  56.3 5.2 %shard_map.86 = (bf16[16,2048]{1,0:T(8,128)(2,1)}, bf16[16,2048]{1,0:T(8,128)(2,1)}, f32[8,16]{1,0:T(8,128)}) custom-call(bf16[16,2048]{1,0:T(8,128)(2,1)} %get-tuple-element.9.refs_0_, bf16[16,2048]{1,0:T(8,128)(2,1)} %get-tuple-element.10.refs_1_, f32[8,16]{1,0:T(8,128)} %get-tuple-element.11.refs_2_), custom_call_target="tpu_custom_call" | custom-call | tf_op jit(solution)/shard_map/pallas_call | solution.py:374

commit v6 on v5

--- a/solution.py
+++ b/solution.py
@@ -322,13 +322,18 @@
 
 
 def deliver_kernel(*refs):
-    sem = refs[-1]
-    half = (len(refs) - 1) // 2
-    copies = [pltpu.make_async_copy(refs[i], refs[half + i], sem.at[i]) for i in range(half)]
-    for copy in copies:
-        copy.start()
-    for copy in copies:
-        copy.wait()
+    count = (len(refs) - 2) // 3
+    load_sem, store_sem = refs[-2:]
+    sources, targets, held = refs[:count], refs[count : 2 * count], refs[2 * count : 3 * count]
+    loads = [pltpu.make_async_copy(sources[i], held[i], load_sem.at[i]) for i in range(count)]
+    stores = [pltpu.make_async_copy(held[i], targets[i], store_sem.at[i]) for i in range(count)]
+    for load in loads:
+        load.start()
+    for load, store in zip(loads, stores):
+        load.wait()
+        store.start()
+    for store in stores:
+        store.wait()
 
 
 def token_shards(tokens, cotangent, gate_probs, expert_ids, up_weight, down_weight):
@@ -376,7 +381,8 @@
         out_shape=tuple(jax.ShapeDtypeStruct(result.shape, result.dtype) for result in results),
         in_specs=[hbm] * len(results),
         out_specs=(hbm,) * len(results),
-        scratch_shapes=[pltpu.SemaphoreType.DMA((len(results),))],
+        scratch_shapes=[pltpu.VMEM(result.shape, result.dtype) for result in results]
+        + [pltpu.SemaphoreType.DMA((len(results),))] * 2,
         compiler_params=pltpu.CompilerParams(vmem_limit_bytes=60 * 1024 * 1024),
     )(*results)
     return mixture, input_grad, gate_grad.T

time: 61.8 us -> 58.1 us (0.940)
  Pallas kernels: 60.9 us -> 57.2 us
    pallas_call x1, Pallas kernels: 5.22 us -> 1.55 us  [token_shards(): pl.pallas_call(deliver_kernel, out_shape=tuple((jax.ShapeDtypeStruct(resu...]
where the time goes in v6:
time: 58.1 us; the launch traced here: 57.9 us
  Pallas kernels  57.2 us (98%)
  between operations  0.64 us (1%)
    pallas_call x1, Pallas kernels, token_shards(): pl.pallas_call(functools.partial(exchange_kernel, experts), out_shape=(ja...  55.7 us
    pallas_call x1, Pallas kernels, token_shards(): pl.pallas_call(deliver_kernel, out_shape=tuple((jax.ShapeDtypeStruct(resu...  1.55 us

profile of v6, /device:TPU:0, one launch (start us, length us, event | category | flops | bytes accessed | tf_op | source)
XLA Modules:
  0.0 57.9 jit_solution(13593609781651553352)
XLA Ops:
  0.6 55.7 %shard_map.85 = (bf16[16,2048]{1,0:T(8,128)(2,1)}, bf16[16,2048]{1,0:T(8,128)(2,1)}, f32[8,16]{1,0:T(8,128)}) custom-call(bf16[16,2048]{1,0:T(8,128)(2,1)} %tokens_hbm.1, bf16[16,2048]{1,0:T(8,128)(2,1)} %cotangent_hbm.1, f32[8,16]{1,0:T(8,128)} %bitcast.3, s32[8,16]{1,0:T(8,128)} %bitcast.4, bf16[1,384,2048]{2,1,0:T(8,128)(2,1)} %up_hbm.1, ...), custom_call_target="tpu_custom_call" | custom-call | tf_op jit(solution)/shard_map/pallas_call | solution.py:348
  56.3 1.6 %shard_map.86 = (bf16[16,2048]{1,0:T(8,128)(2,1)}, bf16[16,2048]{1,0:T(8,128)(2,1)}, f32[8,16]{1,0:T(8,128)}) custom-call(bf16[16,2048]{1,0:T(8,128)(2,1)} %get-tuple-element.9.refs_0_, bf16[16,2048]{1,0:T(8,128)(2,1)} %get-tuple-element.10.refs_1_, f32[8,16]{1,0:T(8,128)} %get-tuple-element.11.refs_2_), custom_call_target="tpu_custom_call" | custom-call | tf_op jit(solution)/shard_map/pallas_call | solution.py:379
